TPU v7x, 256 devices: a whole 4x4x8 slice. The times are simulated.
256 devices in a mesh: section: 8 (over x, z_hi), dp: 4 (over y), tp: 8 (over z_lo, core).
Axes of the slice: x: 4, y: 4, z: 8 (z_hi: 2, z_lo: 4; z = z_hi * 4 + z_lo), core: 2. Of those that a mesh axis runs over, the one named last changes fastest.
Arguments:
- features: bfloat16 [16, 512, 8192], P('section', 'dp', 'tp'), may hold values from -6 to 6
- selected: int32 [3], replicated, may hold values from 0 to 15, as said below
- target_hidden: bfloat16 [512, 8192], P('dp', ('section', 'tp')), may hold values from -6 to 6
- unite_weight: bfloat16 [3, 8192, 8192], P(None, 'tp', 'section')
- head_weight: bfloat16 [65536, 8192], P(('section', 'tp'), 'dp')
Outputs:
- unite_grad: bfloat16 [3, 8192, 8192], P(None, 'tp', ('section', 'dp'))
- kl_loss: float32 [512], P('dp')
Inputs may be any that keep to these rules, and one draw needn't show every extreme that they name: The entries of selected are distinct, and the last one is the deepest offered layer, 15.
All inputs are finite; a program needn't handle non-finite values.
Results may differ from a plain program's by a relative error of at most 0.015.
Values may be sent and summed in bfloat16 or wider, within the bound.
A program may use at most 128 MiB of HBM per device.

v0:
```python
import jax
import jax.numpy as jnp
from jax import lax
from jax.sharding import PartitionSpec as P

D = 8192
LAYERS = 3


EPS = 1e-05


def from_root(value, axis, root):
    mine = lax.axis_index(axis) == root
    return lax.psum(jnp.where(mine, value, jnp.zeros_like(value)), axis)


def contract_rows(left, right):
    return lax.dot_general(
        left, right, (((1,), (1,)), ((), ())), preferred_element_type=jnp.float32
    )


def per_device(features, selected, target_hidden, unite_weight, head_weight):
    offered = features.shape[0]
    picked = []
    for position in range(LAYERS):
        chosen = selected[position]
        local_layer = lax.dynamic_index_in_dim(features, chosen % offered, 0, keepdims=False)
        picked.append(from_root(local_layer, "section", chosen // offered))
    stacked = jnp.stack(picked)
    partial_cols = jnp.einsum(
        "kti,kio->to", stacked, unite_weight, preferred_element_type=jnp.float32
    )
    united_cols = lax.psum_scatter(partial_cols, "tp", scatter_dimension=1, tiled=True)
    squares = lax.psum(jnp.sum(united_cols * united_cols, axis=1), ("section", "tp"))
    scale_inv = lax.rsqrt(squares / D + EPS)[:, None]
    hidden = (united_cols * scale_inv).astype(jnp.bfloat16)
    draft_rows, target_rows = (
        lax.all_gather(hidden, ("section", "tp"), axis=1, tiled=True),
        lax.all_gather(target_hidden, ("section", "tp"), axis=1, tiled=True),
    )
    head_full = lax.all_gather(head_weight, "dp", axis=1, tiled=True)
    target_logits = contract_rows(target_rows, head_full)
    draft_logits = contract_rows(draft_rows, head_full)
    target_peak, draft_peak = lax.pmax(
        (jnp.max(target_logits, axis=1), jnp.max(draft_logits, axis=1)), ("section", "tp")
    )
    target_total, draft_total = lax.psum(
        (
            jnp.sum(jnp.exp(target_logits - target_peak[:, None]), axis=1),
            jnp.sum(jnp.exp(draft_logits - draft_peak[:, None]), axis=1),
        ),
        ("section", "tp"),
    )
    target_log = target_logits - (target_peak + jnp.log(target_total))[:, None]
    draft_log = draft_logits - (draft_peak + jnp.log(draft_total))[:, None]
    target_prob = jnp.exp(target_log)
    draft_prob = jnp.exp(draft_log)
    kl_local = jnp.sum(target_prob * (target_log - draft_log), axis=1)
    kl_loss = lax.psum(kl_local, ("section", "tp"))
    delta_logits = (draft_prob - target_prob).astype(jnp.bfloat16)
    back_part = jnp.dot(delta_logits, head_full, preferred_element_type=jnp.float32)
    back_cols = lax.psum_scatter(back_part, ("section", "tp"), scatter_dimension=1, tiled=True)
    dot_local = jnp.sum(back_cols * united_cols, axis=1)
    dot_sums = lax.psum(dot_local, ("section", "tp"))
    grad_united = (
        scale_inv * back_cols - united_cols * scale_inv**3 * dot_sums[:, None] / D
    ).astype(jnp.bfloat16)
    section_grad = lax.all_gather(grad_united, "tp", axis=1, tiled=True)
    partial_grad = jnp.einsum(
        "kti,to->kio", stacked, section_grad, preferred_element_type=jnp.float32
    )
    weight_grad = lax.psum_scatter(
        partial_grad.astype(jnp.bfloat16), "dp", scatter_dimension=2, tiled=True
    )
    return (weight_grad, kl_loss)


def solution(mesh):
    placed = (
        P("section", "dp", "tp"),
        P(),
        P("dp", ("section", "tp")),
        P(None, "tp", "section"),
        P(("section", "tp"), "dp"),
    )
    return jax.shard_map(
        per_device,
        mesh=mesh,
        in_specs=placed,
        out_specs=(P(None, "tp", ("section", "dp")), P("dp")),
        check_vma=False,
    )
```

profile of v0, /device:TPU:1, one launch (start us, length us, event | category | flops | bytes accessed | tf_op | source)
XLA Modules:
  0.0 1088.7 jit_solution(13770972364516510463)
XLA Ops:
  8.0 0.0 all-reduce.6.cloned.1.call-start
  8.0 1.4 fusion.4
  17.5 2.0 dynamic-slice_select_fusion
  19.5 0.0 all-reduce.6.cloned.1.call-update
  19.5 0.0 reduce-scatter.4.cloned.1.call-start
  19.6 123.1 %all-reduce.6.cloned.1.call-done = (bf16[1,128,1024]{2,1,0:T(8,128)(2,1)}, bf16[1,128,1024]{2,1,0:T(8,128)(2,1)}, bf16[1,128,1024]{2,1,0:T(8,128)(2,1)}) async-done(((bf16[1,128,1024]{2,1,0:T(8,128)(2,1)}, bf16[1,128,1024]{2,1,0:T(8,128)(2,1)}, bf16[1,128,1024]{2,1,0:T(8,128)(2,1)}), (bf16[1,128,1024]{2,1,0:T(8,128)(2,1)}, bf16[1,128,1024]{2,1,0:T(8,128)(2,1)}, ...) | async-done | bytes 786448 | tf_op jit(solution)/shard_map/psum | solution.py:15
  142.7 1.0 constant_dynamic-update-slice_fusion.2
  143.6 1.0 constant_dynamic-update-slice_fusion.1
  144.6 1.0 constant_dynamic-update-slice_fusion
  145.6 4.6 convolution_bitcast_fusion
  150.1 0.0 reduce-scatter.4.cloned.1.call-update
  150.2 0.0 all-gather.8.cloned.1.call-start
  150.2 0.5 all-gather.8.cloned.1.call-update
  150.8 0.0 all-gather.6.cloned.1.call-start
  150.8 0.5 all-gather.6.cloned.1.call-update
  151.3 0.0 all-gather.4.cloned.1.call-start
  151.4 35.5 %reduce-scatter.4.cloned.1.call-done = f32[128,128]{1,0:T(8,128)} async-done(((f32[128,1024]{1,0:T(8,128)}), f32[128,128]{1,0:T(8,128)}) %reduce-scatter.4.cloned.1.call-update) | async-done | bytes 65552 | tf_op jit(solution)/shard_map/reduce_scatter | solution.py:35
  186.8 0.9 multiply_reduce_fusion.2
  187.8 127.4 %psum.59 = f32[128]{0:T(128)S(1)} all-reduce(f32[128]{0:T(128)S(1)} %multiply_reduce_fusion.2), channel_id=1, replica_groups=mesh['section'=8,'dp'=4,'tp'=8] {'section','tp'}, use_global_device_ids=true, to_apply=%region_5.6 | all-reduce | flops 128 | bytes 1024 | tf_op jit(solution)/shard_map/psum | solution.py:36
  315.2 1.5 multiply_convert_fusion
  316.8 0.0 all-gather.4.cloned.1.call-update
  316.8 0.0 reduce-scatter.6.cloned.1.call-start
  316.9 0.0 all-gather.8.cloned.1.call-done
  316.9 69.6 %all-gather.6.cloned.1.call-done = bf16[1024,8192]{1,0:T(8,128)(2,1)} async-done(((bf16[1024,2048]{1,0:T(8,128)(2,1)}), bf16[1024,8192]{1,0:T(8,128)(2,1)}) %all-gather.6.cloned.1.call-update) | async-done | bytes 16777232 | tf_op jit(solution)/shard_map/all_gather | solution.py:43
  386.4 12.2 %fusion.5 = (f32[128]{0:T(128)S(1)}, f32[128,1024]{1,0:T(8,128)S(1)}) fusion(bf16[128,8192]{1,0:T(8,128)(2,1)} %all-gather.8.cloned.1.call-done, bf16[1024,8192]{1,0:T(8,128)(2,1)} %all-gather.6.cloned.1.call-done), kind=kOutput, calls=%fused_computation.25 | convolution fusion | flops 2147614720 | bytes 19399168 | tf_op jit(solution)/shard_map/dot_general | solution.py:19
  398.6 65.0 %all-gather.4.cloned.1.call-done = bf16[128,8192]{1,0:T(8,128)(2,1)} async-done(((bf16[128,128]{1,0:T(8,128)(2,1)}), bf16[128,8192]{1,0:T(8,128)(2,1)}) %all-gather.4.cloned.1.call-update) | async-done | bytes 2097168 | tf_op jit(solution)/shard_map/all_gather | solution.py:40
  463.6 12.2 %fusion.6 = (f32[128]{0:T(128)S(1)}, f32[128,1024]{1,0:T(8,128)S(1)}) fusion(bf16[128,8192]{1,0:T(8,128)(2,1)} %all-gather.4.cloned.1.call-done, bf16[1024,8192]{1,0:T(8,128)(2,1)} %all-gather.6.cloned.1.call-done), kind=kOutput, calls=%fused_computation.26 | convolution fusion | flops 2147614720 | bytes 19399168 | tf_op jit(solution)/shard_map/dot_general | solution.py:19
  475.8 123.7 %all-reduce.2 = (f32[128]{0:T(128)S(1)}, f32[128]{0:T(128)S(1)}) all-reduce(f32[128]{0:T(128)S(1)} %get-tuple-element.19, f32[128]{0:T(128)S(1)} %get-tuple-element.21), channel_id=1, replica_groups=mesh['section'=8,'dp'=4,'tp'=8] {'section','tp'}, use_global_device_ids=true, to_apply=%region_11.12 | all-reduce | flops 256 | bytes 2048 | tf_op jit(solution)/shard_map/pmax | solution.py:46
  599.4 0.3 exponential_reduce_fusion
  599.7 128.8 %all-reduce.1 = (f32[128]{0:T(128)S(1)}, f32[128]{0:T(128)S(1)}) all-reduce(f32[128]{0:T(128)S(1)} %get-tuple-element.23, f32[128]{0:T(128)S(1)} %get-tuple-element.24), channel_id=1, replica_groups=mesh['section'=8,'dp'=4,'tp'=8] {'section','tp'}, use_global_device_ids=true, to_apply=%region_13.14 | all-reduce | flops 256 | bytes 2048 | tf_op jit(solution)/shard_map/psum | solution.py:49
  728.6 0.0 copy-start
  728.6 10.2 fusion
  738.8 0.0 reduce-scatter.6.cloned.1.call-update
  738.8 0.0 reduce-scatter.8.cloned.1.call-start
  738.9 0.3 multiply_reduce_fusion
  739.2 132.2 %reduce-scatter.6.cloned.1.call-done = f32[128,128]{1,0:T(8,128)} async-done(((f32[128,8192]{1,0:T(8,128)}), f32[128,128]{1,0:T(8,128)}) %reduce-scatter.6.cloned.1.call-update) | async-done | bytes 65552 | tf_op jit(solution)/shard_map/reduce_scatter | solution.py:64
  871.3 0.0 copy-done
  871.3 0.9 multiply_reduce_fusion.1
  872.3 129.8 %all-reduce = (f32[128]{0:T(128)S(1)}, f32[128]{0:T(128)}) all-reduce(f32[128]{0:T(128)S(1)} %multiply_reduce_fusion.1, f32[128]{0:T(128)S(1)} %multiply_reduce_fusion), channel_id=1, replica_groups=mesh['section'=8,'dp'=4,'tp'=8] {'section','tp'}, use_global_device_ids=true, to_apply=%region_16.17 | all-reduce | flops 256 | bytes 2048 | tf_op jit(solution)/shard_map/psum | solution.py:66
  1002.1 1.0 subtract_convert_fusion.2
  1003.0 13.6 %all_gather.15 = bf16[128,1024]{1,0:T(8,128)(2,1)S(1)} all-gather(bf16[128,128]{1,0:T(8,128)(2,1)S(1)} %subtract_convert_fusion.2), channel_id=1, replica_groups=mesh['section'=8,'dp'=4,'tp'=8] {'tp'}, dimensions={1}, use_global_device_ids=true | all-gather | bytes 294912 | tf_op jit(solution)/shard_map/all_gather | solution.py:70
  1016.6 4.5 convolution_convert_fusion
  1021.1 0.0 reduce-scatter.8.cloned.1.call-update
  1021.1 60.0 %reduce-scatter.8.cloned.1.call-done = bf16[3,1024,256]{2,1,0:T(8,128)(2,1)} async-done(((bf16[3,1024,1024]{2,1,0:T(8,128)(2,1)}), bf16[3,1024,256]{2,1,0:T(8,128)(2,1)}) %reduce-scatter.8.cloned.1.call-update) | async-done | bytes 1572880 | tf_op jit(solution)/shard_map/reduce_scatter | solution.py:74
  (3 shorter events, 0.0 us)
Async XLA Ops:
  8.0 134.7 %all-reduce.6.cloned.1.call-start = ((), (), s32[]{:S(2)}) async-start(), calls=%async_computation.9 | async-start | bytes 1572864 | tf_op jit(solution)/shard_map/psum | solution.py:15
  19.5 167.3 %reduce-scatter.4.cloned.1.call-start = ((), (), s32[]{:S(2)}) async-start(), calls=%async_computation.3 | async-start | bytes 589824 | tf_op jit(solution)/shard_map/reduce_scatter | solution.py:35
  150.2 166.7 %all-gather.8.cloned.1.call-start = ((), (), s32[]{:S(2)}) async-start(), calls=%async_computation.6 | async-start | bytes 2129920 | tf_op jit(solution)/shard_map/all_gather | solution.py:41
  150.8 235.7 %all-gather.6.cloned.1.call-start = ((), (), s32[]{:S(2)}) async-start(), calls=%async_computation.5 | async-start | bytes 20971520 | tf_op jit(solution)/shard_map/all_gather | solution.py:43
  151.3 312.3 %all-gather.4.cloned.1.call-start = ((), (), s32[]{:S(2)}) async-start(), calls=%async_computation.4 | async-start | bytes 2129920 | tf_op jit(solution)/shard_map/all_gather | solution.py:40
  316.8 554.5 %reduce-scatter.6.cloned.1.call-start = ((), (), s32[]{:S(2)}) async-start(), calls=%async_computation.7 | async-start | bytes 4259840 | tf_op jit(solution)/shard_map/reduce_scatter | solution.py:64
  728.6 142.8 %copy-start = (f32[128,128]{1,0:T(8,128)S(1)}, f32[128,128]{1,0:T(8,128)}, u32[]{:S(2)}) copy-start(f32[128,128]{1,0:T(8,128)} %reduce-scatter.4.cloned.1.call-done) | copy-start | bytes 196612
  738.8 342.3 %reduce-scatter.8.cloned.1.call-start = ((), (), s32[]{:S(2)}) async-start(), calls=%async_computation.8 | async-start | bytes 7864320 | tf_op jit(solution)/shard_map/reduce_scatter | solution.py:74
Sparse Core Ops, SparseCore 0:
  19.7 122.9 all-reduce.5
  150.3 36.5 reduce-scatter.3
Sparse Core Ops, SparseCore 1:
  153.2 76.5 all-gather.7
  231.4 155.0 all-gather.5
  389.5 74.1 all-gather.3
  738.9 132.4 reduce-scatter.5
  1021.2 59.8 reduce-scatter.7
where the time goes:
time: 1090 us
  blocking collectives  523 us (48%)
  waiting for transfers between devices  486 us (45%)
  matrix products  43.6 us (4%)
  between operations  23.8 us (2%)
    reduce_scatter x1, waiting for transfers between devices, per_device(): lax.psum_scatter(back_part, ('section', 'tp'), scatter_dimension=1, tiled...  132 us
    psum x1, blocking collectives, per_device(): dot_sums = lax.psum(dot_local, ('section', 'tp'))  130 us
    psum x1, blocking collectives, per_device(): lax.psum((jnp.sum(jnp.exp(target_logits - target_peak[:, None]), axis=1),...  129 us
    psum x1, blocking collectives, per_device(): lax.psum(jnp.sum(united_cols * united_cols, axis=1), ('section', 'tp'))  127 us
    pmax x1, blocking collectives, per_device(): lax.pmax((jnp.max(target_logits, axis=1), jnp.max(draft_logits, axis=1)),...  124 us
    psum x1, waiting for transfers between devices, from_root(): return lax.psum(jnp.where(mine, value, jnp.zeros_like(value)), axis)  123 us
    all_gather x1, waiting for transfers between devices, per_device(): head_full = lax.all_gather(head_weight, 'dp', axis=1, tiled=True)  69.6 us
    all_gather x1, waiting for transfers between devices, per_device(): lax.all_gather(hidden, ('section', 'tp'), axis=1, tiled=True)  65 us
  transfers between devices with their start and end apart: 7, of which 6 were waited for; matrix products, arithmetic and copies ran while one was open for 1% of the time, Pallas kernels for 0%

commit v1 on v0

v1 whole, which is shorter than its diff:
```python
import jax
import jax.numpy as jnp
from jax import lax
from jax.experimental import pallas as pl
from jax.experimental.pallas import tpu as pltpu
from jax.sharding import PartitionSpec as P

D = 8192
LAYERS = 3
EPS = 1e-05
BF = jnp.bfloat16
F32 = jnp.float32
NSEM = 256


def nt(a, b):
    return lax.dot_general(a, b, (((1,), (1,)), ((), ())), preferred_element_type=F32)


def nn(a, b):
    return jnp.dot(a, b, preferred_element_type=F32)


def rows_to_cols(tile):
    return jnp.concatenate([tile, jnp.zeros((120, 128), F32)], axis=0).T


def combine(parts):
    row = lax.broadcasted_iota(jnp.int32, (8, 128), 0)
    upper = row < 4

    def spread(p):
        return jnp.where(upper, p[0:1, :], p[4:5, :])

    peaks = [spread(p) for p in parts]
    peak = peaks[0]
    for other in peaks[1:]:
        peak = jnp.maximum(peak, other)
    total = jnp.zeros((8, 128), F32)
    for p, mine in zip(parts, peaks):
        total = total + p * jnp.exp(mine - peak)
    return jnp.where((row == 0) | (row == 4), peak, total)


def kernel(
    sel, feat_h, tgt_h, w_h, head_h, out_h, kl_o,
    feat, tgt, w, head, msk, fx, fs, fz, fall, ft,
    part, pc, pz, uni, ssc, ssz, ssa, ssx, scol, tcol,
    h_t, h_d, lp_t, lp_d, lq_t, lq_d, rq_t, rq_d, sm, sq_t, sq_d, rs_t, rs_d,
    zt, zd, stat, stc, stz, stx, fin, fcol, dall,
    bk, rc, bx, rx, rz, bs, ur, gcol, gu, outv,
    lsem, send, recv,
):
    sec = lax.axis_index("section")
    y = lax.axis_index("dp")
    tp = lax.axis_index("tp")
    x, zh = lax.div(sec, 2), lax.rem(sec, 2)
    zl, c = lax.div(tp, 2), lax.rem(tp, 2)
    z = zh * 4 + zl
    oc = 1 - c

    def mod4(v):
        return lax.rem(v + 8, 4)

    def to_x(v):
        return {"section": v * 2 + zh}

    def to_y(v):
        return {"dp": v}

    def to_z(v):
        return {"section": x * 2 + lax.div(v, 4), "tp": lax.rem(v, 4) * 2 + c}

    sibling = {"tp": zl * 2 + oc}
    across = {"section": y * 2 + zh, "dp": x}

    def across_z(v):
        return {"section": y * 2 + lax.div(v, 4), "dp": x, "tp": lax.rem(v, 4) * 2 + c}

    def turned(h):
        return {"section": y * 2 + zh, "dp": zl, "tp": x * 2 + h}

    def turned_back(h):
        return {"section": zl * 2 + zh, "dp": x, "tp": y * 2 + h}

    counter = [0]

    def sems(n):
        base = counter[0]
        counter[0] += n
        assert counter[0] <= NSEM
        return base

    ends = []

    def copy(src, dst, sem, dev, rsem=None):
        return pltpu.make_async_remote_copy(
            src_ref=src, dst_ref=dst, send_sem=send.at[sem],
            recv_sem=recv.at[sem if rsem is None else rsem],
            device_id=dev, device_id_type=pl.DeviceIdType.MESH,
        )

    def push(src, dst, sem, dev, rsem=None, when=None):
        if when is None:
            copy(src, dst, sem, dev, rsem).start()
            ends.append(lambda: copy(src, dst, sem, dev, rsem).wait_send())
        else:
            def go():
                copy(src, dst, sem, dev, rsem).start()

            def end():
                copy(src, dst, sem, dev, rsem).wait_send()

            pl.when(when)(go)
            ends.append(lambda: pl.when(when)(end))

    def await_recv(dst, sem, when=None):
        def go():
            copy(dst, dst, 0, sibling, sem).wait_recv()

        if when is None:
            go()
        else:
            pl.when(when)(go)

    def m(v, k):
        return pl.multiple_of(v, k)

    half_c = pl.ds(m(c * 128, 128), 128)
    half_o = pl.ds(m(oc * 128, 128), 128)

    loads = [
        pltpu.make_async_copy(feat_h, feat, lsem.at[0]),
        pltpu.make_async_copy(tgt_h, tgt, lsem.at[1]),
        pltpu.make_async_copy(w_h, w, lsem.at[2]),
        pltpu.make_async_copy(head_h, head, lsem.at[3]),
    ]
    for load in loads:
        load.start()

    barrier = pltpu.get_barrier_semaphore()

    def greet(dev):
        pl.semaphore_signal(barrier, inc=1, device_id=dev, device_id_type=pl.DeviceIdType.MESH)

    for d in range(1, 4):
        greet(to_x(mod4(x + d)))
        greet(to_y(mod4(y + d)))
    for d in range(1, 8):
        greet(to_z(lax.rem(z + d, 8)))
    greet(sibling)
    off_x = x != y
    off_z = jnp.logical_or(off_x, y != zl)

    @pl.when(off_x)
    def _():
        for v in range(8):
            greet(across_z(v))

    @pl.when(off_z)
    def _():
        for h in range(2):
            greet(turned(h))
            greet(turned_back(h))

    pl.semaphore_wait(
        barrier, 14 + jnp.where(off_x, 8, 0) + jnp.where(off_z, 4, 0)
    )

    class Gather:
        def __init__(self, hid, own):
            self.hid, self.own = hid, own
            self.s1, self.sz, self.sx = sems(1), sems(8), sems(8)
            self.so, self.sf = sems(2), sems(8)

        def turn(self):
            hid, own = self.hid, self.own
            push(own, hid.at[y, z, :, half_c], self.s1, across, when=off_x)

            @pl.when(jnp.logical_not(off_x))
            def _():
                hid[x, z, :, half_c] = own[...]

        def along_z(self):
            hid = self.hid
            mine = hid.at[x, z, :, half_c]
            if self.own is not None:
                await_recv(mine, self.s1, when=off_x)
            for d in range(1, 8):
                push(mine, mine, self.sz + d, to_z(lax.rem(z + d, 8)))

        def along_x(self, g):
            hid = self.hid
            base = zh * 4 if g == 0 else 4 - zh * 4
            for j in range(1 if g == 0 else 0, 4):
                zz = base + mod4(zl + j)
                await_recv(hid.at[x, zz, :, half_c], self.sz + lax.rem(z - zz + 8, 8))
            block = hid.at[x, pl.ds(base, 4), :, half_c]
            for d in (1, 3, 2):
                push(block, block, self.sx + g * 4 + d, to_x(mod4(x + d)))
            push(block, block, self.so + g, sibling)

        def over(self, g):
            hid = self.hid
            base = zh * 4 if g == 0 else 4 - zh * 4
            for d in (1, 3, 2):
                block = hid.at[mod4(x - d), pl.ds(base, 4), :, half_c]
                await_recv(block, self.sx + g * 4 + d)
                push(block, block, self.sf + g * 4 + d, sibling)

        def finish(self):
            hid = self.hid
            for g in range(2):
                base = zh * 4 if g == 0 else 4 - zh * 4
                await_recv(hid.at[x, pl.ds(base, 4), :, half_o], self.so + g)
                for d in (1, 3, 2):
                    block = hid.at[mod4(x - d), pl.ds(base, 4), :, half_o]
                    await_recv(block, self.sf + g * 4 + d)

    class Logits:
        def __init__(self, hid, lp, lq, rq, sq, rs):
            self.hid, self.lp, self.lq, self.rq, self.sq, self.rs = hid, lp, lq, rq, sq, rs
            self.s, self.ss = sems(4), sems(4)

        def product(self, rels):
            hid, lp = self.hid, self.lp

            @pl.loop(0, 4)
            def _(n):
                cols = pl.ds(m(n * 256, 256), 256)
                left = jnp.concatenate(
                    [jnp.concatenate([hid[mod4(y + rel), i] for i in range(8)], axis=1) for rel in rels],
                    axis=0,
                )
                out = nt(left, head[cols, :])
                for j, rel in enumerate(rels):
                    lp[rel, :, cols] = out[j * 128:(j + 1) * 128]

        def send(self, rel):
            lp, lq, sq = self.lp, self.lq, self.sq

            @pl.loop(0, 4)
            def _(i):
                rows = pl.ds(m(i * 32, 32), 32)
                v = lp[rel, rows]
                peak = jnp.maximum(jnp.max(jnp.abs(v), axis=1, keepdims=True), 1e-30)
                lq[rel, rows] = jnp.round(v * (32767.0 / peak)).astype(jnp.int32).astype(jnp.int16)
                sm[rows] = jnp.broadcast_to(peak / 32767.0, (32, 128))

            sq[rel] = sm[...].T[0:8]
            dev = to_y(mod4(y + rel))
            push(lq.at[rel], self.rq.at[rel], self.s + rel, dev)
            push(sq.at[rel], self.rs.at[rel], self.ss + rel, dev)

        def finish(self, col, other):
            for rel in (1, 3, 2):
                await_recv(self.rs.at[rel], self.ss + rel)
            row = lax.broadcasted_iota(jnp.int32, (8, 128), 0)
            tile = other
            for rel in (1, 3, 2):
                tile = jnp.where(row == rel, self.rs[rel], tile)
            col[...] = rows_to_cols(tile)
            for rel in (1, 3, 2):
                await_recv(self.rq.at[rel], self.s + rel)

        def total(self, col, rows):
            out = self.lp[0, rows]
            for rel in (1, 3, 2):
                part_sum = self.rq[rel, rows].astype(jnp.int32).astype(F32)
                out = out + part_sum * col[rows, rel:rel + 1]
            return out

    target = Gather(h_t, tgt)
    draft = Gather(h_d, None)
    logits_t = Logits(h_t, lp_t, lq_t, rq_t, sq_t, rs_t)
    logits_d = Logits(h_d, lp_d, lq_d, rq_d, sq_d, rs_d)

    loads[1].wait()
    target.turn()
    loads[0].wait()
    f1, f2, f3, f4, f5 = sems(12), sems(3), sems(12), sems(12), sems(12)
    for k in range(LAYERS):
        chosen = sel[k]
        value = feat[lax.rem(chosen, 2)]
        mine = lax.div(chosen, 2) == sec
        msk[k] = jnp.where(mine, value, jnp.zeros_like(value))
        for d in (1, 3, 2):
            xx = mod4(x + d)
            push(msk.at[k, pl.ds(m(xx * 32, 32), 32)], fx.at[k, d - 1], f1 + k * 4 + d, to_x(xx))
    quarter = pl.ds(m(x * 32, 32), 32)
    other_zh = {"section": x * 2 + 1 - zh}
    for k in range(LAYERS):
        for d in (1, 3, 2):
            await_recv(fx.at[k, d - 1], f1 + k * 4 + d)
        fs[k] = msk[k, quarter] + fx[k, 0] + fx[k, 1] + fx[k, 2]
        push(fs.at[k], fz.at[k], f2 + k, other_zh)
    target.along_z()
    for k in range(LAYERS):
        await_recv(fz.at[k], f2 + k)
        fall[y, k, quarter] = fs[k] + fz[k]
        block = fall.at[y, k, quarter]
        for d in (1, 3, 2):
            push(block, block, f3 + k * 4 + d, to_x(mod4(x + d)))
            push(block, block, f4 + k * 4 + d, to_y(mod4(y + d)))

    loads[2].wait()
    for k in range(LAYERS):
        for d in (1, 3, 2):
            xx = mod4(x - d)
            await_recv(fall.at[y, k, pl.ds(m(xx * 32, 32), 32)], f3 + k * 4 + d)
        if k == LAYERS - 1:
            target.along_x(0)
            target.along_x(1)

        @pl.loop(0, 4)
        def _(n, k=k):
            cols = pl.ds(m(n * 256, 256), 256)
            term = nn(fall[y, k], w[k, :, cols])
            if k:
                part[n, 0] = part[n, 0] + term[:, :128]
                part[n, 1] = part[n, 1] + term[:, 128:]
            else:
                part[n, 0] = term[:, :128]
                part[n, 1] = term[:, 128:]

    r1, r2 = sems(1), sems(4)
    push(part.at[:, oc], pc, r1, sibling)
    await_recv(pc, r1)
    for d in (2, 1, 3, 0):
        v = mod4(zl + d)
        part[v, c] = part[v, c] + pc[v]
        remote = off_x if d == 0 else None
        push(part.at[v, c], pz.at[zl], r2 + d, across_z(zh * 4 + v), rsem=r2 + zl, when=remote)

    @pl.when(jnp.logical_not(off_x))
    def _():
        pz[zl] = part[zl, c]

    for d in range(4):
        v = mod4(zl + d)
        await_recv(pz.at[v], r2 + v, when=off_x if d == 0 else None)
    uni[...] = pz[0] + pz[1] + pz[2] + pz[3]
    h_d[x, z, :, half_c] = uni[...].astype(BF)
    draft.along_z()
    s_c, s_z, s_a, s_x = sems(1), sems(8), sems(1), sems(4)
    squares = jnp.sum(uni[...] * uni[...], axis=1, keepdims=True)
    ssc[0] = jnp.broadcast_to(squares, (128, 128)).T[0:8]
    push(ssc.at[0], ssc.at[1], s_c, sibling)
    t2 = sems(2)
    for h in range(2):
        src = uni.at[pl.ds(h * 64, 64), :]
        push(src, ur.at[:, half_c], t2 + h, turned(h), rsem=t2 + c,
             when=jnp.logical_or(off_z, c != h))

    @pl.when(jnp.logical_not(off_z))
    def _():
        ur[:, half_c] = uni[pl.ds(m(c * 64, 64), 64), :]

    target.over(0)
    target.over(1)
    await_recv(ssc.at[1], s_c)
    ssz[0] = ssc[0] + ssc[1]
    for d in range(1, 8):
        push(ssz.at[0], ssz.at[d], s_z + d, to_z(lax.rem(z + d, 8)))
    draft.along_x(0)
    draft.along_x(1)
    target.finish()
    loads[3].wait()
    logits_t.product((1, 3, 2, 0))
    for rel in (2, 1, 3):
        logits_t.send(rel)
    for d in range(1, 8):
        await_recv(ssz.at[d], s_z + d)
    total = ssz[0]
    for d in range(1, 8):
        total = total + ssz[d]
    ssa[0] = total
    push(ssa.at[0], ssa.at[1], s_a, across, when=off_x)
    draft.over(0)
    draft.over(1)
    await_recv(ssa.at[1], s_a, when=off_x)
    ssx[0] = jnp.where(off_x, ssa[1], ssa[0])
    for d in range(1, 4):
        push(ssx.at[0], ssx.at[d], s_x + d, to_x(mod4(x + d)))
    draft.finish()
    for e in (1, 3, 2):
        yy = mod4(y - e)
        for k in range(LAYERS):
            await_recv(fall.at[yy, k, quarter], f4 + k * 4 + e)
        block = fall.at[yy, :, quarter]
        for d in (1, 3, 2):
            push(block, block, f5 + (e - 1) * 4 + d, to_x(mod4(x + d)))
    logits_d.product((1, 3))
    logits_d.send(1)
    logits_d.send(3)
    logits_d.product((2, 0))
    logits_d.send(2)
    def transpose(b):
        @pl.loop(0, LAYERS)
        def _(k):
            for i in range(4):
                ft[k, pl.ds(i * 256, 256), pl.ds(m(b * 128, 128), 128)] = fall[b, k, :, pl.ds(i * 256, 256)].T

    transpose(y)
    logits_t.finish(tcol, jnp.zeros((8, 128), F32))

    @pl.loop(0, 4)
    def _(i):
        rows = pl.ds(m(i * 32, 32), 32)
        zt[rows] = logits_t.total(tcol, rows)

    for d in range(1, 4):
        await_recv(ssx.at[d], s_x + d)
    scale_rows = lax.rsqrt((ssx[0] + ssx[1] + ssx[2] + ssx[3]) / D + EPS)
    logits_d.finish(scol, scale_rows)

    @pl.loop(0, 4)
    def _(i):
        rows = pl.ds(m(i * 32, 32), 32)
        a = zt[rows]
        b = logits_d.total(scol, rows) * scol[rows, 0:1]
        zd[rows] = b
        ma = jnp.max(a, axis=1, keepdims=True)
        mb = jnp.max(b, axis=1, keepdims=True)
        ea, eb = jnp.exp(a - ma), jnp.exp(b - mb)

        def total(v):
            return jnp.sum(v, axis=1, keepdims=True)

        values = [ma, total(ea), total(ea * (a - b)), total(ea * b), mb, total(eb), total(eb * b)]
        spot = lax.broadcasted_iota(jnp.int32, (32, 128), 1)
        out = jnp.zeros((32, 128), F32)
        for j, v in enumerate(values):
            out = jnp.where(spot == j, v, out)
        stat[rows] = out

    q_c, q_z, q_x, q_y = sems(1), sems(8), sems(4), sems(4)
    stc[0] = stat[...].T[0:8]
    push(stc.at[0], stc.at[1], q_c, sibling)
    await_recv(stc.at[1], q_c)
    stz[0] = combine([stc[0], stc[1]])
    for d in range(1, 8):
        push(stz.at[0], stz.at[d], q_z + d, to_z(lax.rem(z + d, 8)))
    for d in range(1, 8):
        await_recv(stz.at[d], q_z + d)
    stx[0] = combine([stz[d] for d in range(8)])
    for d in range(1, 4):
        push(stx.at[0], stx.at[d], q_x + d, to_x(mod4(x + d)))
    for d in range(1, 4):
        await_recv(stx.at[d], q_x + d)
    all_stats = combine([stx[d] for d in range(4)])
    log_t = all_stats[0:1] + jnp.log(all_stats[1:2])
    log_d = all_stats[4:5] + jnp.log(all_stats[5:6])
    kl_o[...] = all_stats[2:3] / all_stats[1:2] - log_t + log_d
    energy = all_stats[6:7] / all_stats[5:6] - all_stats[3:4] / all_stats[1:2]
    row = lax.broadcasted_iota(jnp.int32, (8, 128), 0)
    tile = jnp.where(row == 0, log_t, jnp.where(row == 1, log_d, jnp.where(row == 2, scale_rows[0:1], energy)))
    fin[y] = tile
    fcol[...] = rows_to_cols(tile)

    @pl.loop(0, 4)
    def _(i):
        rows = pl.ds(m(i * 32, 32), 32)
        pt = jnp.exp(zt[rows] - fcol[rows, 0:1])
        pd = jnp.exp(zd[rows] - fcol[rows, 1:2])
        dall[y, rows] = (pd - pt).astype(BF)

    d1 = sems(4)
    for d in (1, 3, 2):
        push(dall.at[y], dall.at[y], d1 + d, to_y(mod4(y + d)))
    for d in range(1, 4):
        push(fin.at[y], fin.at[y], q_y + d, to_y(mod4(y + d)))

    b_c, b_x, b_z = sems(4), sems(16), sems(8)

    def product(rels):
        for rel in rels:
            if rel:
                b = mod4(y + rel)
                await_recv(dall.at[b], d1 + 4 - rel)

        @pl.loop(0, 8)
        def _(n):
            cols = pl.ds(m(n * 256, 256), 256)
            left = jnp.concatenate([dall[mod4(y + rel)] for rel in rels], axis=0)
            out = nn(left, head[:, cols]).astype(BF)
            for j, rel in enumerate(rels):
                bk[rel, :, cols] = out[j * 128:(j + 1) * 128]

        for rel in rels:
            push(bk.at[rel, pl.ds(m(oc * 64, 64), 64)], rc.at[rel], b_c + rel, sibling)

    def over_core(rel):
        await_recv(rc.at[rel], b_c + rel)
        mine = pl.ds(m(c * 64, 64), 64)
        for n in range(8):
            cols = pl.ds(n * 256, 256)
            s = bk[rel, mine, cols].astype(F32) + rc[rel, :, cols].astype(F32)
            bx[rel, n % 4, n // 4] = s.astype(BF)
        for d in (1, 3, 2):
            xx = mod4(x + d)
            push(bx.at[rel, xx], rx.at[rel, d - 1], b_x + rel * 4 + d, to_x(xx))

    def over_x(rel):
        b = mod4(y + rel)
        for d in (1, 3, 2):
            await_recv(rx.at[rel, d - 1], b_x + rel * 4 + d)
        s = bx[rel, x].astype(F32)
        for d in range(3):
            s = s + rx[rel, d].astype(F32)
        bs[rel] = s.astype(BF)
        for g in range(2):
            zz = g * 4 + b
            push(bs.at[rel, g], rz.at[z], b_z + rel * 2 + g, across_z(zz), rsem=b_z + z,
                 when=jnp.logical_or(off_x, zz != z))

            @pl.when(jnp.logical_not(jnp.logical_or(off_x, zz != z)))
            def _():
                rz[z] = bs[rel, g]

    product((0,))
    over_core(0)
    product((1, 3))
    over_core(1)
    over_core(3)
    over_x(0)
    product((2,))
    over_core(2)
    over_x(1)
    over_x(3)
    over_x(2)

    for d in range(1, 4):
        await_recv(fin.at[mod4(y - d)], q_y + d)
    gcol[...] = rows_to_cols(fin[zl])
    await_recv(ur.at[:, pl.ds(0, 128)], t2, when=jnp.logical_or(off_z, c != 0))
    await_recv(ur.at[:, pl.ds(128, 128)], t2 + 1, when=jnp.logical_or(off_z, c != 1))
    for e in (1, 3, 2):
        yy = mod4(y - e)
        for d in (1, 3, 2):
            xx = mod4(x - d)
            await_recv(fall.at[yy, :, pl.ds(m(xx * 32, 32), 32)], f5 + (e - 1) * 4 + d)
        transpose(yy)
    for d in range(8):
        zz = lax.rem(z + d, 8)
        await_recv(rz.at[zz], b_z + zz, when=off_x if d == 0 else None)
    bt = rz[0].astype(F32)
    for j in range(1, 8):
        bt = bt + rz[j].astype(F32)
    mine = pl.ds(m(c * 64, 64), 64)
    scale = gcol[mine, 2:3]
    gu[zl, c] = (scale * (bt - ur[...] * (scale * gcol[mine, 3:4] / D))).astype(BF)

    g1, g2 = sems(4), sems(4)
    for d in (0, 1, 3, 2):
        if d:
            block = gu.at[zl, c]
            push(block, block, g1 + d, {"tp": mod4(zl + d) * 2 + c})
    for d in (0, 1, 3, 2):
        v = mod4(zl - d)
        block = gu.at[v, c]
        if d:
            await_recv(block, g1 + d)
        push(block, block, g2 + d, sibling)
    for d in (0, 1, 3, 2):
        await_recv(gu.at[mod4(zl - d), oc], g2 + d)

    stores = []
    for k in range(LAYERS):
        @pl.loop(0, 4)
        def _(i, k=k):
            rows = pl.ds(m(i * 256, 256), 256)
            right = jnp.concatenate([gu[b, h] for b in range(4) for h in range(2)], axis=0)
            outv[k, rows] = nn(ft[k, rows], right).astype(BF)

        store = pltpu.make_async_copy(outv.at[k], out_h.at[k], lsem.at[4 + k])
        store.start()
        stores.append(store)
    for end in ends:
        end()
    for store in stores:
        store.wait()


def per_device(features, selected, target_hidden, unite_weight, head_weight):
    def vm(shape, kind):
        return pltpu.VMEM(shape, kind)

    scratch = [
        vm((2, 128, 1024), BF), vm((128, 128), BF), vm((3, 1024, 1024), BF), vm((1024, 2048), BF),
        vm((3, 128, 1024), BF), vm((3, 3, 32, 1024), BF), vm((3, 32, 1024), BF), vm((3, 32, 1024), BF),
        vm((4, 3, 128, 1024), BF), vm((3, 1024, 512), BF),
        vm((4, 2, 128, 128), F32), vm((4, 128, 128), F32), vm((4, 128, 128), F32), vm((128, 128), F32),
        vm((2, 8, 128), F32), vm((8, 8, 128), F32), vm((2, 8, 128), F32), vm((4, 8, 128), F32),
        vm((128, 128), F32), vm((128, 128), F32),
        vm((4, 8, 128, 256), BF), vm((4, 8, 128, 256), BF),
        vm((4, 128, 1024), F32), vm((4, 128, 1024), F32),
        vm((4, 128, 1024), jnp.int16), vm((4, 128, 1024), jnp.int16),
        vm((4, 128, 1024), jnp.int16), vm((4, 128, 1024), jnp.int16), vm((128, 128), F32),
        vm((4, 8, 128), F32), vm((4, 8, 128), F32), vm((4, 8, 128), F32), vm((4, 8, 128), F32),
        vm((128, 1024), F32), vm((128, 1024), F32), vm((128, 128), F32),
        vm((2, 8, 128), F32), vm((8, 8, 128), F32), vm((4, 8, 128), F32),
        vm((4, 8, 128), F32), vm((128, 128), F32), vm((4, 128, 1024), BF),
        vm((4, 128, 2048), BF), vm((4, 64, 2048), BF), vm((4, 4, 2, 64, 256), BF),
        vm((4, 3, 2, 64, 256), BF), vm((8, 64, 256), BF), vm((4, 2, 64, 256), BF),
        vm((64, 256), F32), vm((128, 128), F32),
        vm((4, 2, 64, 256), BF), vm((3, 1024, 256), BF),
        pltpu.SemaphoreType.DMA((8,)), pltpu.SemaphoreType.DMA((NSEM,)), pltpu.SemaphoreType.DMA((NSEM,)),
    ]
    anywhere = pl.BlockSpec(memory_space=pl.ANY)
    grad, loss = pl.pallas_call(
        kernel,
        out_shape=(
            jax.ShapeDtypeStruct((3, 1024, 256), BF),
            jax.ShapeDtypeStruct((1, 128), F32),
        ),
        in_specs=[pl.BlockSpec(memory_space=pltpu.SMEM)] + [anywhere] * 4,
        out_specs=(anywhere, pl.BlockSpec(memory_space=pltpu.VMEM)),
        scratch_shapes=scratch,
        compiler_params=pltpu.CompilerParams(
            collective_id=0, has_side_effects=True, vmem_limit_bytes=58 * 1024 * 1024
        ),
    )(selected, features, target_hidden, unite_weight, head_weight)
    return grad, loss.reshape(128)


def solution(mesh):
    placed = (
        P("section", "dp", "tp"),
        P(),
        P("dp", ("section", "tp")),
        P(None, "tp", "section"),
        P(("section", "tp"), "dp"),
    )
    return jax.shard_map(
        per_device,
        mesh=mesh,
        in_specs=placed,
        out_specs=(P(None, "tp", ("section", "dp")), P("dp")),
        check_vma=False,
    )
```

time: 1090 us -> 171 us (0.16)
  blocking collectives: 523 us -> 0 us
  waiting for transfers between devices: 486 us -> 0 us
  Pallas kernels: 0 us -> 166 us
  matrix products: 43.6 us -> 0 us
  between operations: 23.8 us -> 0.64 us
    psum x3 -> x0, blocking collectives: 386 us -> none  [the longest x1 130 us: per_device(): dot_sums = lax.psum(dot_local, ('section', 'tp'))]
    reduce_scatter x3 -> x0, waiting for transfers between devices: 228 us -> none  [the longest x1 132 us: per_device(): lax.psum_scatter(back_part, ('section', 'tp'), scatter_dimension=1, tiled...]
    pallas_call x0 -> x1, Pallas kernels: none -> 166 us  [per_device(): pl.pallas_call(kernel, out_shape=(jax.ShapeDtypeStruct((3, 1024, 256), BF...]
    all_gather x3 -> x0, waiting for transfers between devices: 135 us -> none  [the longest x1 69.6 us: per_device(): head_full = lax.all_gather(head_weight, 'dp', axis=1, tiled=True)]
    pmax x1 -> x0, blocking collectives: 124 us -> none  [per_device(): lax.pmax((jnp.max(target_logits, axis=1), jnp.max(draft_logits, axis=1)),...]
    psum x1 -> x0, waiting for transfers between devices: 123 us -> none  [from_root(): return lax.psum(jnp.where(mine, value, jnp.zeros_like(value)), axis)]
    dot_general x5 -> x0, matrix products: 43.6 us -> none  [the longest x2 24.3 us: contract_rows(): lax.dot_general(left, right, (((1,), (1,)), ((), ())), preferred_element_...]
    all_gather x1 -> x0, blocking collectives: 13.6 us -> none  [per_device(): section_grad = lax.all_gather(grad_united, 'tp', axis=1, tiled=True)]
  transfers between devices with their start and end apart: 7 -> 0, of which waited for: 6 -> 0; matrix products, arithmetic and copies ran while one was open for 1% -> 0% of each run, Pallas kernels for 0% -> 0%
where the time goes in v1:
time: 171 us
  Pallas kernels  166 us (97%)
  local copies, waits for them, and re-layouts  3.83 us (2%)
    pallas_call x1, Pallas kernels, per_device(): pl.pallas_call(kernel, out_shape=(jax.ShapeDtypeStruct((3, 1024, 256), BF...  166 us
    unnamed x2, local copies, waits for them, and re-layouts  3.83 us

profile of v1, /device:TPU:1, one launch (start us, length us, event | category | flops | bytes accessed | tf_op | source)
XLA Modules:
  0.0 170.7 jit_solution(12682768182761155653)
XLA Ops:
  0.6 166.3 %shard_map.68 = (bf16[3,1024,256]{2,1,0:T(8,128)(2,1)}, f32[1,128]{1,0:T(1,128)}) custom-call(s32[3]{0:T(128)} %sel.1, bf16[2,128,1024]{2,1,0:T(8,128)(2,1)} %feat_h.1, bf16[128,128]{1,0:T(8,128)(2,1)} %tgt_h.1, bf16[3,1024,1024]{2,1,0:T(8,128)(2,1)} %w_h.1, bf16[1024,2048]{1,0:T(8,128)(2,1)} %head_h.1), custom_call_target="tpu_custom_call" | custom-call | tf_op jit(solution)/shard_map/pallas_call | solution.py:611
  166.9 2.7 %copy.9 = bf16[3,1024,256]{2,1,0:T(8,128)(2,1)} copy(bf16[3,1024,256]{2,1,0:T(8,128)(2,1)} %get-tuple-element.8) | data formatting | bytes 3145728
  169.5 1.2 copy.10

commit v2 on v1

--- a/solution.py
+++ b/solution.py
@@ -43,12 +43,12 @@
 
 
 def kernel(
-    sel, feat_h, tgt_h, w_h, head_h, out_h, kl_o,
+    sel, feat_h, tgt_h, w_h, head_h, ft_h, gu_h, kl_o,
     feat, tgt, w, head, msk, fx, fs, fz, fall, ft,
     part, pc, pz, uni, ssc, ssz, ssa, ssx, scol, tcol,
     h_t, h_d, lp_t, lp_d, lq_t, lq_d, rq_t, rq_d, sm, sq_t, sq_d, rs_t, rs_d,
-    zt, zd, stat, stc, stz, stx, fin, fcol, dall,
-    bk, rc, bx, rx, rz, bs, ur, gcol, gu, outv,
+    zt, zd, stat, stc, stz, stx, ste, fin, fcol, dall,
+    bk, rc, bx, rx, rz, bs, bsum, bturn, ur, gcol, gu,
     lsem, send, recv,
 ):
     sec = lax.axis_index("section")
@@ -72,16 +72,23 @@
         return {"section": x * 2 + lax.div(v, 4), "tp": lax.rem(v, 4) * 2 + c}
 
     sibling = {"tp": zl * 2 + oc}
-    across = {"section": y * 2 + zh, "dp": x}
-
-    def across_z(v):
-        return {"section": y * 2 + lax.div(v, 4), "dp": x, "tp": lax.rem(v, 4) * 2 + c}
+    group = mod4(x - y)
+
+    def there(v):
+        return {"section": mod4(x + y) * 2 + lax.div(v, 4), "dp": x, "tp": lax.rem(v, 4) * 2 + c}
+
+    def back_to(v):
+        return {"section": y * 2 + lax.div(v, 4), "dp": group, "tp": lax.rem(v, 4) * 2 + c}
+
+    def far(d, j):
+        zz = lax.rem(z + c + 2 * j, 8)
+        return {"section": mod4(x + d) * 2 + lax.div(zz, 4), "tp": lax.rem(zz, 4) * 2 + c}
 
     def turned(h):
-        return {"section": y * 2 + zh, "dp": zl, "tp": x * 2 + h}
+        return {"section": y * 2 + zh, "dp": zl, "tp": group * 2 + h}
 
     def turned_back(h):
-        return {"section": zl * 2 + zh, "dp": x, "tp": y * 2 + h}
+        return {"section": mod4(x + zl) * 2 + zh, "dp": x, "tp": y * 2 + h}
 
     counter = [0]
 
@@ -149,13 +156,14 @@
     for d in range(1, 8):
         greet(to_z(lax.rem(z + d, 8)))
     greet(sibling)
-    off_x = x != y
-    off_z = jnp.logical_or(off_x, y != zl)
+    off_x = jnp.logical_or(x != 0, y != 0)
+    off_z = jnp.logical_or(off_x, zl != 0)
 
     @pl.when(off_x)
     def _():
-        for v in range(8):
-            greet(across_z(v))
+        for v in range(4):
+            greet(there(zh * 4 + v))
+            greet(back_to(zh * 4 + v))
 
     @pl.when(off_z)
     def _():
@@ -163,8 +171,20 @@
             greet(turned(h))
             greet(turned_back(h))
 
+    @pl.when(c == 0)
+    def _():
+        for d in range(1, 4):
+            for j in range(1, 4):
+                greet(far(d, j))
+
+    @pl.when(c == 1)
+    def _():
+        for d in range(1, 4):
+            for j in range(4):
+                greet(far(d, j))
+
     pl.semaphore_wait(
-        barrier, 14 + jnp.where(off_x, 8, 0) + jnp.where(off_z, 4, 0)
+        barrier, 23 + 3 * c + jnp.where(off_x, 8, 0) + jnp.where(off_z, 4, 0)
     )
 
     class Gather:
@@ -172,102 +192,123 @@
             self.hid, self.own = hid, own
             self.s1, self.sz, self.sx = sems(1), sems(8), sems(8)
             self.so, self.sf = sems(2), sems(8)
+            self.s2, self.sz2 = sems(1), sems(8)
 
         def turn(self):
             hid, own = self.hid, self.own
-            push(own, hid.at[y, z, :, half_c], self.s1, across, when=off_x)
+            push(own, hid.at[y, z, :, half_c], self.s1, there(z), when=off_x)
 
             @pl.when(jnp.logical_not(off_x))
             def _():
-                hid[x, z, :, half_c] = own[...]
+                hid[group, z, :, half_c] = own[...]
 
         def along_z(self):
-            hid = self.hid
-            mine = hid.at[x, z, :, half_c]
+            mine = self.hid.at[group, z, :, half_c]
             if self.own is not None:
                 await_recv(mine, self.s1, when=off_x)
             for d in range(1, 8):
                 push(mine, mine, self.sz + d, to_z(lax.rem(z + d, 8)))
 
-        def along_x(self, g):
-            hid = self.hid
+        def hop(self):
+            piece = self.hid.at[group, z, :, half_c]
+            push(piece, piece, self.s2, to_x(mod4(x + 2)))
+
+        def hop_z(self):
+            piece = self.hid.at[mod4(group + 2), z, :, half_c]
+            await_recv(piece, self.s2)
+            for d in range(1, 8):
+                push(piece, piece, self.sz2 + d, to_z(lax.rem(z + d, 8)))
+
+        def hop_over(self):
+            for d in range(1, 8):
+                await_recv(self.hid.at[mod4(group + 2), lax.rem(z + 8 - d, 8), :, half_c], self.sz2 + d)
+            for g in range(2):
+                block = self.block(2, g, half_c)
+                push(block, block, self.sf + g * 4 + 2, sibling)
+
+        def block(self, e, g, half):
+            base = zh * 4 if g == 0 else 4 - zh * 4
+            return self.hid.at[mod4(group + e), pl.ds(base, 4), :, half]
+
+        def await_z(self, g):
             base = zh * 4 if g == 0 else 4 - zh * 4
             for j in range(1 if g == 0 else 0, 4):
                 zz = base + mod4(zl + j)
-                await_recv(hid.at[x, zz, :, half_c], self.sz + lax.rem(z - zz + 8, 8))
-            block = hid.at[x, pl.ds(base, 4), :, half_c]
-            for d in (1, 3, 2):
+                await_recv(self.hid.at[group, zz, :, half_c], self.sz + lax.rem(z - zz + 8, 8))
+
+        def along_x(self, g, steps):
+            block = self.block(0, g, half_c)
+            for d in steps:
                 push(block, block, self.sx + g * 4 + d, to_x(mod4(x + d)))
+
+        def own_over(self, g):
+            block = self.block(0, g, half_c)
             push(block, block, self.so + g, sibling)
 
-        def over(self, g):
-            hid = self.hid
-            base = zh * 4 if g == 0 else 4 - zh * 4
-            for d in (1, 3, 2):
-                block = hid.at[mod4(x - d), pl.ds(base, 4), :, half_c]
-                await_recv(block, self.sx + g * 4 + d)
-                push(block, block, self.sf + g * 4 + d, sibling)
-
-        def finish(self):
-            hid = self.hid
+        def over(self, g, e):
+            block = self.block(e, g, half_c)
+            await_recv(block, self.sx + g * 4 + 4 - e)
+            push(block, block, self.sf + g * 4 + e, sibling)
+
+        def finish(self, e):
             for g in range(2):
-                base = zh * 4 if g == 0 else 4 - zh * 4
-                await_recv(hid.at[x, pl.ds(base, 4), :, half_o], self.so + g)
-                for d in (1, 3, 2):
-                    block = hid.at[mod4(x - d), pl.ds(base, 4), :, half_o]
-                    await_recv(block, self.sf + g * 4 + d)
+                await_recv(self.block(e, g, half_o), self.sf + g * 4 + e if e else self.so + g)
 
     class Logits:
         def __init__(self, hid, lp, lq, rq, sq, rs):
             self.hid, self.lp, self.lq, self.rq, self.sq, self.rs = hid, lp, lq, rq, sq, rs
             self.s, self.ss = sems(4), sems(4)
 
-        def product(self, rels):
+        def product(self, steps):
             hid, lp = self.hid, self.lp
 
             @pl.loop(0, 4)
             def _(n):
                 cols = pl.ds(m(n * 256, 256), 256)
                 left = jnp.concatenate(
-                    [jnp.concatenate([hid[mod4(y + rel), i] for i in range(8)], axis=1) for rel in rels],
+                    [jnp.concatenate([hid[mod4(group + e), i] for i in range(8)], axis=1) for e in steps],
                     axis=0,
                 )
                 out = nt(left, head[cols, :])
-                for j, rel in enumerate(rels):
-                    lp[rel, :, cols] = out[j * 128:(j + 1) * 128]
-
-        def send(self, rel):
+                for j, e in enumerate(steps):
+                    lp[e, :, cols] = out[j * 128:(j + 1) * 128]
+
+        def send(self, e):
             lp, lq, sq = self.lp, self.lq, self.sq
-
-            @pl.loop(0, 4)
-            def _(i):
-                rows = pl.ds(m(i * 32, 32), 32)
-                v = lp[rel, rows]
-                peak = jnp.maximum(jnp.max(jnp.abs(v), axis=1, keepdims=True), 1e-30)
-                lq[rel, rows] = jnp.round(v * (32767.0 / peak)).astype(jnp.int32).astype(jnp.int16)
-                sm[rows] = jnp.broadcast_to(peak / 32767.0, (32, 128))
-
-            sq[rel] = sm[...].T[0:8]
-            dev = to_y(mod4(y + rel))
-            push(lq.at[rel], self.rq.at[rel], self.s + rel, dev)
-            push(sq.at[rel], self.rs.at[rel], self.ss + rel, dev)
+            b = mod4(group + e)
+
+            @pl.when(b != y)
+            def _():
+                @pl.loop(0, 4)
+                def _(i):
+                    rows = pl.ds(m(i * 32, 32), 32)
+                    v = lp[e, rows]
+                    peak = jnp.maximum(jnp.max(jnp.abs(v), axis=1, keepdims=True), 1e-30)
+                    lq[e, rows] = jnp.round(v * (32767.0 / peak)).astype(jnp.int32).astype(jnp.int16)
+                    sm[rows] = jnp.broadcast_to(peak / 32767.0, (32, 128))
+
+                sq[e] = sm[...].T[0:8]
+
+            push(lq.at[e], self.rq.at[y], self.s + e, to_y(b), rsem=self.s + y, when=b != y)
+            push(sq.at[e], self.rs.at[y], self.ss + e, to_y(b), rsem=self.ss + y, when=b != y)
 
         def finish(self, col, other):
-            for rel in (1, 3, 2):
-                await_recv(self.rs.at[rel], self.ss + rel)
             row = lax.broadcasted_iota(jnp.int32, (8, 128), 0)
             tile = other
-            for rel in (1, 3, 2):
-                tile = jnp.where(row == rel, self.rs[rel], tile)
+            for e in (1, 3, 2):
+                yy = mod4(y - e)
+                await_recv(self.rs.at[yy], self.ss + yy)
+                tile = jnp.where(row == e, self.rs[yy], tile)
             col[...] = rows_to_cols(tile)
-            for rel in (1, 3, 2):
-                await_recv(self.rq.at[rel], self.s + rel)
+            for e in (1, 3, 2):
+                yy = mod4(y - e)
+                await_recv(self.rq.at[yy], self.s + yy)
 
         def total(self, col, rows):
-            out = self.lp[0, rows]
-            for rel in (1, 3, 2):
-                part_sum = self.rq[rel, rows].astype(jnp.int32).astype(F32)
-                out = out + part_sum * col[rows, rel:rel + 1]
+            out = self.lp[mod4(y - group), rows]
+            for e in (1, 3, 2):
+                term = self.rq[mod4(y - e), rows].astype(jnp.int32).astype(F32)
+                out = out + term * col[rows, e:e + 1]
             return out
 
     target = Gather(h_t, tgt)
@@ -287,6 +328,8 @@
         for d in (1, 3, 2):
             xx = mod4(x + d)
             push(msk.at[k, pl.ds(m(xx * 32, 32), 32)], fx.at[k, d - 1], f1 + k * 4 + d, to_x(xx))
+    target.along_z()
+    target.hop()
     quarter = pl.ds(m(x * 32, 32), 32)
     other_zh = {"section": x * 2 + 1 - zh}
     for k in range(LAYERS):
@@ -294,23 +337,28 @@
             await_recv(fx.at[k, d - 1], f1 + k * 4 + d)
         fs[k] = msk[k, quarter] + fx[k, 0] + fx[k, 1] + fx[k, 2]
         push(fs.at[k], fz.at[k], f2 + k, other_zh)
-    target.along_z()
+    target.hop_z()
     for k in range(LAYERS):
         await_recv(fz.at[k], f2 + k)
         fall[y, k, quarter] = fs[k] + fz[k]
         block = fall.at[y, k, quarter]
         for d in (1, 3, 2):
             push(block, block, f3 + k * 4 + d, to_x(mod4(x + d)))
-            push(block, block, f4 + k * 4 + d, to_y(mod4(y + d)))
+            if k:
+                push(block, block, f4 + k * 4 + d, to_y(mod4(y + d)))
+    for g in range(2):
+        target.await_z(g)
+        target.along_x(g, (1, 3))
+        target.own_over(g)
 
     loads[2].wait()
     for k in range(LAYERS):
         for d in (1, 3, 2):
             xx = mod4(x - d)
             await_recv(fall.at[y, k, pl.ds(m(xx * 32, 32), 32)], f3 + k * 4 + d)
-        if k == LAYERS - 1:
-            target.along_x(0)
-            target.along_x(1)
+        if k == 0:
+            for d in (1, 3, 2):
+                push(fall.at[y, 0], fall.at[y, 0], f4 + d, to_y(mod4(y + d)))
 
         @pl.loop(0, 4)
         def _(n, k=k):
@@ -330,7 +378,7 @@
         v = mod4(zl + d)
         part[v, c] = part[v, c] + pc[v]
         remote = off_x if d == 0 else None
-        push(part.at[v, c], pz.at[zl], r2 + d, across_z(zh * 4 + v), rsem=r2 + zl, when=remote)
+        push(part.at[v, c], pz.at[zl], r2 + d, there(zh * 4 + v), rsem=r2 + zl, when=remote)
 
     @pl.when(jnp.logical_not(off_x))
     def _():
@@ -340,8 +388,9 @@
         v = mod4(zl + d)
         await_recv(pz.at[v], r2 + v, when=off_x if d == 0 else None)
     uni[...] = pz[0] + pz[1] + pz[2] + pz[3]
-    h_d[x, z, :, half_c] = uni[...].astype(BF)
+    h_d[group, z, :, half_c] = uni[...].astype(BF)
     draft.along_z()
+    draft.hop()
     s_c, s_z, s_a, s_x = sems(1), sems(8), sems(1), sems(4)
     squares = jnp.sum(uni[...] * uni[...], axis=1, keepdims=True)
     ssc[0] = jnp.broadcast_to(squares, (128, 128)).T[0:8]
@@ -356,50 +405,70 @@
     def _():
         ur[:, half_c] = uni[pl.ds(m(c * 64, 64), 64), :]
 
-    target.over(0)
-    target.over(1)
     await_recv(ssc.at[1], s_c)
     ssz[0] = ssc[0] + ssc[1]
     for d in range(1, 8):
         push(ssz.at[0], ssz.at[d], s_z + d, to_z(lax.rem(z + d, 8)))
-    draft.along_x(0)
-    draft.along_x(1)
-    target.finish()
+    draft.hop_z()
+    target.hop_over()
+    for g in range(2):
+        for e in (1, 3):
+            target.over(g, e)
+    for e in range(4):
+        target.finish(e)
     loads[3].wait()
-    logits_t.product((1, 3, 2, 0))
-    for rel in (2, 1, 3):
-        logits_t.send(rel)
+    logits_t.product((0, 1, 3, 2))
+    for g in range(2):
+        draft.await_z(g)
+        draft.along_x(g, (1, 3))
+        draft.own_over(g)
+    for e in (0, 1, 3, 2):
+        logits_t.send(e)
     for d in range(1, 8):
         await_recv(ssz.at[d], s_z + d)
     total = ssz[0]
     for d in range(1, 8):
         total = total + ssz[d]
     ssa[0] = total
-    push(ssa.at[0], ssa.at[1], s_a, across, when=off_x)
-    draft.over(0)
-    draft.over(1)
+    push(ssa.at[0], ssa.at[1], s_a, back_to(z), when=off_x)
+    draft.finish(0)
+    logits_d.product((0,))
+    logits_d.send(0)
+    for g in range(2):
+        for e in (1, 3):
+            draft.over(g, e)
+    draft.hop_over()
     await_recv(ssa.at[1], s_a, when=off_x)
     ssx[0] = jnp.where(off_x, ssa[1], ssa[0])
     for d in range(1, 4):
         push(ssx.at[0], ssx.at[d], s_x + d, to_x(mod4(x + d)))
-    draft.finish()
-    for e in (1, 3, 2):
+
+    def foreign(e):
         yy = mod4(y - e)
-        for k in range(LAYERS):
+        for k in (1, 2):
             await_recv(fall.at[yy, k, quarter], f4 + k * 4 + e)
-        block = fall.at[yy, :, quarter]
+        block = fall.at[yy, pl.ds(1, 2), quarter]
         for d in (1, 3, 2):
             push(block, block, f5 + (e - 1) * 4 + d, to_x(mod4(x + d)))
+
+    foreign(1)
+    foreign(3)
+    draft.finish(1)
+    draft.finish(3)
     logits_d.product((1, 3))
     logits_d.send(1)
     logits_d.send(3)
-    logits_d.product((2, 0))
+    draft.finish(2)
+    logits_d.product((2,))
     logits_d.send(2)
+    foreign(2)
     def transpose(b):
         @pl.loop(0, LAYERS)
         def _(k):
             for i in range(4):
-                ft[k, pl.ds(i * 256, 256), pl.ds(m(b * 128, 128), 128)] = fall[b, k, :, pl.ds(i * 256, 256)].T
+                ft[b, k, pl.ds(i * 256, 256)] = fall[b, k, :, pl.ds(i * 256, 256)].T
+
+        pltpu.make_async_copy(ft.at[b], ft_h.at[b], lsem.at[4 + b]).start()
 
     transpose(y)
     logits_t.finish(tcol, jnp.zeros((8, 128), F32))
@@ -434,21 +503,26 @@
             out = jnp.where(spot == j, v, out)
         stat[rows] = out
 
-    q_c, q_z, q_x, q_y = sems(1), sems(8), sems(4), sems(4)
+    q_c, q_f, q_e, q_y = sems(1), sems(16), sems(1), sems(4)
     stc[0] = stat[...].T[0:8]
     push(stc.at[0], stc.at[1], q_c, sibling)
     await_recv(stc.at[1], q_c)
-    stz[0] = combine([stc[0], stc[1]])
-    for d in range(1, 8):
-        push(stz.at[0], stz.at[d], q_z + d, to_z(lax.rem(z + d, 8)))
-    for d in range(1, 8):
-        await_recv(stz.at[d], q_z + d)
-    stx[0] = combine([stz[d] for d in range(8)])
-    for d in range(1, 4):
-        push(stx.at[0], stx.at[d], q_x + d, to_x(mod4(x + d)))
-    for d in range(1, 4):
-        await_recv(stx.at[d], q_x + d)
-    all_stats = combine([stx[d] for d in range(4)])
+    stz[...] = combine([stc[0], stc[1]])
+    for d in range(4):
+        for j in range(4):
+            push(stz, stx.at[d, j], q_f + d * 4 + j, far(d, j), when=c == 1 if d + j == 0 else None)
+
+    @pl.when(c == 0)
+    def _():
+        stx[0, 0] = stz[...]
+
+    for d in range(4):
+        for j in range(4):
+            await_recv(stx.at[d, j], q_f + d * 4 + j, when=c == 1 if d + j == 0 else None)
+    ste[0] = combine([stx[d, j] for d in range(4) for j in range(4)])
+    push(ste.at[0], ste.at[1], q_e, sibling)
+    await_recv(ste.at[1], q_e)
+    all_stats = combine([ste[0], ste[1]])
     log_t = all_stats[0:1] + jnp.log(all_stats[1:2])
     log_d = all_stats[4:5] + jnp.log(all_stats[5:6])
     kl_o[...] = all_stats[2:3] / all_stats[1:2] - log_t + log_d
@@ -499,22 +573,21 @@
             bx[rel, n % 4, n // 4] = s.astype(BF)
         for d in (1, 3, 2):
             xx = mod4(x + d)
-            push(bx.at[rel, xx], rx.at[rel, d - 1], b_x + rel * 4 + d, to_x(xx))
+            push(bx.at[rel, mod4(xx - y)], rx.at[rel, d - 1], b_x + rel * 4 + d, to_x(xx))
 
     def over_x(rel):
         b = mod4(y + rel)
         for d in (1, 3, 2):
             await_recv(rx.at[rel, d - 1], b_x + rel * 4 + d)
-        s = bx[rel, x].astype(F32)
+        s = bx[rel, group].astype(F32)
         for d in range(3):
             s = s + rx[rel, d].astype(F32)
         bs[rel] = s.astype(BF)
         for g in range(2):
             zz = g * 4 + b
-            push(bs.at[rel, g], rz.at[z], b_z + rel * 2 + g, across_z(zz), rsem=b_z + z,
-                 when=jnp.logical_or(off_x, zz != z))
-
-            @pl.when(jnp.logical_not(jnp.logical_or(off_x, zz != z)))
+            push(bs.at[rel, g], rz.at[z], b_z + rel * 2 + g, to_z(zz), rsem=b_z + z, when=zz != z)
+
+            @pl.when(zz == z)
             def _():
                 rz[z] = bs[rel, g]
 
@@ -537,16 +610,27 @@
     await_recv(ur.at[:, pl.ds(128, 128)], t2 + 1, when=jnp.logical_or(off_z, c != 1))
     for e in (1, 3, 2):
         yy = mod4(y - e)
+        await_recv(fall.at[yy, 0], f4 + e)
         for d in (1, 3, 2):
             xx = mod4(x - d)
-            await_recv(fall.at[yy, :, pl.ds(m(xx * 32, 32), 32)], f5 + (e - 1) * 4 + d)
+            await_recv(fall.at[yy, pl.ds(1, 2), pl.ds(m(xx * 32, 32), 32)], f5 + (e - 1) * 4 + d)
         transpose(yy)
-    for d in range(8):
+    for d in range(1, 8):
         zz = lax.rem(z + d, 8)
-        await_recv(rz.at[zz], b_z + zz, when=off_x if d == 0 else None)
-    bt = rz[0].astype(F32)
+        await_recv(rz.at[zz], b_z + zz)
+    total = rz[0].astype(F32)
     for j in range(1, 8):
-        bt = bt + rz[j].astype(F32)
+        total = total + rz[j].astype(F32)
+    bsum[...] = total.astype(BF)
+    t1 = sems(1)
+    push(bsum, bturn, t1, back_to(z), when=off_x)
+
+    @pl.when(jnp.logical_not(off_x))
+    def _():
+        bturn[...] = bsum[...]
+
+    await_recv(bturn, t1, when=off_x)
+    bt = bturn[...].astype(F32)
     mine = pl.ds(m(c * 64, 64), 64)
     scale = gcol[mine, 2:3]
     gu[zl, c] = (scale * (bt - ur[...] * (scale * gcol[mine, 3:4] / D))).astype(BF)
@@ -565,21 +649,20 @@
     for d in (0, 1, 3, 2):
         await_recv(gu.at[mod4(zl - d), oc], g2 + d)
 
-    stores = []
-    for k in range(LAYERS):
-        @pl.loop(0, 4)
-        def _(i, k=k):
-            rows = pl.ds(m(i * 256, 256), 256)
-            right = jnp.concatenate([gu[b, h] for b in range(4) for h in range(2)], axis=0)
-            outv[k, rows] = nn(ft[k, rows], right).astype(BF)
-
-        store = pltpu.make_async_copy(outv.at[k], out_h.at[k], lsem.at[4 + k])
-        store.start()
-        stores.append(store)
+    store = pltpu.make_async_copy(gu, gu_h, lsem.at[8])
+    store.start()
     for end in ends:
         end()
-    for store in stores:
-        store.wait()
+    store.wait()
+    for b in range(4):
+        pltpu.make_async_copy(ft.at[b], ft_h.at[b], lsem.at[4 + b]).wait()
+
+
+def outer(ft, gu, loss, out, loss_out):
+    left = jnp.concatenate([ft[b, 0] for b in range(4)], axis=1)
+    right = jnp.concatenate([gu[b, h] for b in range(4) for h in range(2)], axis=0)
+    out[0] = nn(left, right).astype(BF)
+    loss_out[...] = loss[...]
 
 
 def per_device(features, selected, target_hidden, unite_weight, head_weight):
@@ -589,7 +672,7 @@
     scratch = [
         vm((2, 128, 1024), BF), vm((128, 128), BF), vm((3, 1024, 1024), BF), vm((1024, 2048), BF),
         vm((3, 128, 1024), BF), vm((3, 3, 32, 1024), BF), vm((3, 32, 1024), BF), vm((3, 32, 1024), BF),
-        vm((4, 3, 128, 1024), BF), vm((3, 1024, 512), BF),
+        vm((4, 3, 128, 1024), BF), vm((4, 3, 1024, 128), BF),
         vm((4, 2, 128, 128), F32), vm((4, 128, 128), F32), vm((4, 128, 128), F32), vm((128, 128), F32),
         vm((2, 8, 128), F32), vm((8, 8, 128), F32), vm((2, 8, 128), F32), vm((4, 8, 128), F32),
         vm((128, 128), F32), vm((128, 128), F32),
@@ -599,28 +682,47 @@
         vm((4, 128, 1024), jnp.int16), vm((4, 128, 1024), jnp.int16), vm((128, 128), F32),
         vm((4, 8, 128), F32), vm((4, 8, 128), F32), vm((4, 8, 128), F32), vm((4, 8, 128), F32),
         vm((128, 1024), F32), vm((128, 1024), F32), vm((128, 128), F32),
-        vm((2, 8, 128), F32), vm((8, 8, 128), F32), vm((4, 8, 128), F32),
+        vm((2, 8, 128), F32), vm((8, 128), F32), vm((4, 4, 8, 128), F32), vm((2, 8, 128), F32),
         vm((4, 8, 128), F32), vm((128, 128), F32), vm((4, 128, 1024), BF),
         vm((4, 128, 2048), BF), vm((4, 64, 2048), BF), vm((4, 4, 2, 64, 256), BF),
         vm((4, 3, 2, 64, 256), BF), vm((8, 64, 256), BF), vm((4, 2, 64, 256), BF),
-        vm((64, 256), F32), vm((128, 128), F32),
-        vm((4, 2, 64, 256), BF), vm((3, 1024, 256), BF),
-        pltpu.SemaphoreType.DMA((8,)), pltpu.SemaphoreType.DMA((NSEM,)), pltpu.SemaphoreType.DMA((NSEM,)),
+        vm((64, 256), BF), vm((64, 256), BF), vm((64, 256), F32), vm((128, 128), F32),
+        vm((4, 2, 64, 256), BF),
+        pltpu.SemaphoreType.DMA((9,)), pltpu.SemaphoreType.DMA((NSEM,)), pltpu.SemaphoreType.DMA((NSEM,)),
     ]
     anywhere = pl.BlockSpec(memory_space=pl.ANY)
-    grad, loss = pl.pallas_call(
+    turned, grad_united, loss = pl.pallas_call(
         kernel,
         out_shape=(
-            jax.ShapeDtypeStruct((3, 1024, 256), BF),
+            jax.ShapeDtypeStruct((4, 3, 1024, 128), BF),
+            jax.ShapeDtypeStruct((4, 2, 64, 256), BF),
             jax.ShapeDtypeStruct((1, 128), F32),
         ),
         in_specs=[pl.BlockSpec(memory_space=pltpu.SMEM)] + [anywhere] * 4,
-        out_specs=(anywhere, pl.BlockSpec(memory_space=pltpu.VMEM)),
+        out_specs=(anywhere, anywhere, pl.BlockSpec(memory_space=pltpu.VMEM)),
         scratch_shapes=scratch,
         compiler_params=pltpu.CompilerParams(
             collective_id=0, has_side_effects=True, vmem_limit_bytes=58 * 1024 * 1024
         ),
     )(selected, features, target_hidden, unite_weight, head_weight)
+    grad, loss = pl.pallas_call(
+        outer,
+        grid=(LAYERS,),
+        out_shape=(
+            jax.ShapeDtypeStruct((3, 1024, 256), BF),
+            jax.ShapeDtypeStruct((1, 128), F32),
+        ),
+        in_specs=[
+            pl.BlockSpec((4, 1, 1024, 128), lambda k: (0, k, 0, 0)),
+            pl.BlockSpec((4, 2, 64, 256), lambda k: (0, 0, 0, 0)),
+            pl.BlockSpec((1, 128), lambda k: (0, 0)),
+        ],
+        out_specs=(
+            pl.BlockSpec((1, 1024, 256), lambda k: (k, 0, 0)),
+            pl.BlockSpec((1, 128), lambda k: (0, 0)),
+        ),
+        compiler_params=pltpu.CompilerParams(vmem_limit_bytes=60 * 1024 * 1024),
+    )(turned, grad_united, loss)
     return grad, loss.reshape(128)
 
 

time: 171 us -> 155 us (0.906); the launches traced: 171 us -> 153 us
  Pallas kernels: 166 us -> 152 us
  local copies, waits for them, and re-layouts: 3.83 us -> 0 us
    pallas_call x1 -> x2, Pallas kernels: 166 us -> 152 us  [the longest x1 147 us: per_device(): pl.pallas_call(kernel, out_shape=(jax.ShapeDtypeStruct((4, 3, 1024, 128),...]
    unnamed x2 -> x0, local copies, waits for them, and re-layouts: 3.83 us -> none
where the time goes in v2:
time: 155 us; the launch traced here: 153 us
  Pallas kernels  152 us (98%)
    pallas_call x1, Pallas kernels, per_device(): pl.pallas_call(kernel, out_shape=(jax.ShapeDtypeStruct((4, 3, 1024, 128),...  147 us
    pallas_call x1, Pallas kernels, per_device(): pl.pallas_call(outer, grid=(LAYERS,), out_shape=(jax.ShapeDtypeStruct((3,...  4.51 us

profile of v2, /device:TPU:1, one launch (start us, length us, event | category | flops | bytes accessed | tf_op | source)
XLA Modules:
  0.0 152.6 jit_solution(10239996152064654271)
XLA Ops:
  0.6 147.5 %shard_map.68 = (bf16[4,3,1024,128]{3,2,1,0:T(8,128)(2,1)}, bf16[4,2,64,256]{3,2,1,0:T(8,128)(2,1)}, f32[1,128]{1,0:T(1,128)}) custom-call(s32[3]{0:T(128)} %sel.1, bf16[2,128,1024]{2,1,0:T(8,128)(2,1)} %feat_h.1, bf16[128,128]{1,0:T(8,128)(2,1)} %tgt_h.1, bf16[3,1024,1024]{2,1,0:T(8,128)(2,1)} %w_h.1, bf16[1024,2048]{1,0:T(8,128)(2,1)} %head_h.1), custom_call_target="tpu_custom_call" | custom-call | tf_op jit(solution)/shard_map/pallas_call | solution.py:694
  148.1 4.5 %shard_map.69 = (bf16[3,1024,256]{2,1,0:T(8,128)(2,1)}, f32[1,128]{1,0:T(1,128)}) custom-call(bf16[4,3,1024,128]{3,2,1,0:T(8,128)(2,1)} %get-tuple-element.7.ft, bf16[4,2,64,256]{3,2,1,0:T(8,128)(2,1)} %get-tuple-element.8.gu, f32[1,128]{1,0:T(1,128)} %get-tuple-element.9.loss), custom_call_target="tpu_custom_call" | custom-call | tf_op jit(solution)/shard_map/pallas_call | solution.py:708

commit v3 on v2

--- a/solution.py
+++ b/solution.py
@@ -328,8 +328,6 @@
         for d in (1, 3, 2):
             xx = mod4(x + d)
             push(msk.at[k, pl.ds(m(xx * 32, 32), 32)], fx.at[k, d - 1], f1 + k * 4 + d, to_x(xx))
-    target.along_z()
-    target.hop()
     quarter = pl.ds(m(x * 32, 32), 32)
     other_zh = {"section": x * 2 + 1 - zh}
     for k in range(LAYERS):
@@ -337,7 +335,8 @@
             await_recv(fx.at[k, d - 1], f1 + k * 4 + d)
         fs[k] = msk[k, quarter] + fx[k, 0] + fx[k, 1] + fx[k, 2]
         push(fs.at[k], fz.at[k], f2 + k, other_zh)
-    target.hop_z()
+    target.along_z()
+    target.hop()
     for k in range(LAYERS):
         await_recv(fz.at[k], f2 + k)
         fall[y, k, quarter] = fs[k] + fz[k]
@@ -346,10 +345,7 @@
             push(block, block, f3 + k * 4 + d, to_x(mod4(x + d)))
             if k:
                 push(block, block, f4 + k * 4 + d, to_y(mod4(y + d)))
-    for g in range(2):
-        target.await_z(g)
-        target.along_x(g, (1, 3))
-        target.own_over(g)
+    target.hop_z()
 
     loads[2].wait()
     for k in range(LAYERS):
@@ -360,8 +356,7 @@
             for d in (1, 3, 2):
                 push(fall.at[y, 0], fall.at[y, 0], f4 + d, to_y(mod4(y + d)))
 
-        @pl.loop(0, 4)
-        def _(n, k=k):
+        def unite(n, k):
             cols = pl.ds(m(n * 256, 256), 256)
             term = nn(fall[y, k], w[k, :, cols])
             if k:
@@ -371,11 +366,17 @@
                 part[n, 0] = term[:, :128]
                 part[n, 1] = term[:, 128:]
 
-    r1, r2 = sems(1), sems(4)
-    push(part.at[:, oc], pc, r1, sibling)
-    await_recv(pc, r1)
+        if k < LAYERS - 1:
+            pl.loop(0, 4)(lambda n, k=k: unite(n, k))
+
+    r1, r2 = sems(4), sems(4)
     for d in (2, 1, 3, 0):
         v = mod4(zl + d)
+        unite(v, LAYERS - 1)
+        push(part.at[v, oc], pc.at[v], r1 + d, sibling)
+    for d in (2, 1, 3, 0):
+        v = mod4(zl + d)
+        await_recv(pc.at[v], r1 + d)
         part[v, c] = part[v, c] + pc[v]
         remote = off_x if d == 0 else None
         push(part.at[v, c], pz.at[zl], r2 + d, there(zh * 4 + v), rsem=r2 + zl, when=remote)
@@ -384,6 +385,14 @@
     def _():
         pz[zl] = part[zl, c]
 
+    for g in range(2):
+        target.await_z(g)
+        target.along_x(g, (1, 3))
+        target.own_over(g)
+    loads[3].wait()
+    target.finish(0)
+    logits_t.product((0,))
+    logits_t.send(0)
     for d in range(4):
         v = mod4(zl + d)
         await_recv(pz.at[v], r2 + v, when=off_x if d == 0 else None)
@@ -395,16 +404,6 @@
     squares = jnp.sum(uni[...] * uni[...], axis=1, keepdims=True)
     ssc[0] = jnp.broadcast_to(squares, (128, 128)).T[0:8]
     push(ssc.at[0], ssc.at[1], s_c, sibling)
-    t2 = sems(2)
-    for h in range(2):
-        src = uni.at[pl.ds(h * 64, 64), :]
-        push(src, ur.at[:, half_c], t2 + h, turned(h), rsem=t2 + c,
-             when=jnp.logical_or(off_z, c != h))
-
-    @pl.when(jnp.logical_not(off_z))
-    def _():
-        ur[:, half_c] = uni[pl.ds(m(c * 64, 64), 64), :]
-
     await_recv(ssc.at[1], s_c)
     ssz[0] = ssc[0] + ssc[1]
     for d in range(1, 8):
@@ -414,15 +413,14 @@
     for g in range(2):
         for e in (1, 3):
             target.over(g, e)
-    for e in range(4):
+    for e in (1, 3, 2):
         target.finish(e)
-    loads[3].wait()
-    logits_t.product((0, 1, 3, 2))
+    logits_t.product((1, 3, 2))
     for g in range(2):
         draft.await_z(g)
         draft.along_x(g, (1, 3))
         draft.own_over(g)
-    for e in (0, 1, 3, 2):
+    for e in (1, 3, 2):
         logits_t.send(e)
     for d in range(1, 8):
         await_recv(ssz.at[d], s_z + d)
@@ -434,10 +432,13 @@
     draft.finish(0)
     logits_d.product((0,))
     logits_d.send(0)
+    draft.hop_over()
+    draft.finish(2)
+    logits_d.product((2,))
+    logits_d.send(2)
     for g in range(2):
         for e in (1, 3):
             draft.over(g, e)
-    draft.hop_over()
     await_recv(ssa.at[1], s_a, when=off_x)
     ssx[0] = jnp.where(off_x, ssa[1], ssa[0])
     for d in range(1, 4):
@@ -458,10 +459,17 @@
     logits_d.product((1, 3))
     logits_d.send(1)
     logits_d.send(3)
-    draft.finish(2)
-    logits_d.product((2,))
-    logits_d.send(2)
     foreign(2)
+    t2 = sems(2)
+    for h in range(2):
+        src = uni.at[pl.ds(h * 64, 64), :]
+        push(src, ur.at[:, half_c], t2 + h, turned(h), rsem=t2 + c,
+             when=jnp.logical_or(off_z, c != h))
+
+    @pl.when(jnp.logical_not(off_z))
+    def _():
+        ur[:, half_c] = uni[pl.ds(m(c * 64, 64), 64), :]
+
     def transpose(b):
         @pl.loop(0, LAYERS)
         def _(k):
@@ -540,8 +548,9 @@
         dall[y, rows] = (pd - pt).astype(BF)
 
     d1 = sems(4)
-    for d in (1, 3, 2):
-        push(dall.at[y], dall.at[y], d1 + d, to_y(mod4(y + d)))
+    near = [copy(dall.at[y], dall.at[y], d1 + d, to_y(mod4(y + d))) for d in (1, 3)]
+    for sent in near:
+        sent.start()
     for d in range(1, 4):
         push(fin.at[y], fin.at[y], q_y + d, to_y(mod4(y + d)))
 
@@ -593,6 +602,9 @@
 
     product((0,))
     over_core(0)
+    for sent in near:
+        sent.wait_send()
+    push(dall.at[y], dall.at[y], d1 + 2, to_y(mod4(y + 2)))
     product((1, 3))
     over_core(1)
     over_core(3)

time: 155 us -> 150 us (0.968)
  Pallas kernels: 152 us -> 147 us
    pallas_call x1, Pallas kernels: 147 us -> 143 us  [per_device(): pl.pallas_call(kernel, out_shape=(jax.ShapeDtypeStruct((4, 3, 1024, 128),...]
where the time goes in v3:
time: 150 us; the launch traced here: 148 us
  Pallas kernels  147 us (98%)
    pallas_call x1, Pallas kernels, per_device(): pl.pallas_call(kernel, out_shape=(jax.ShapeDtypeStruct((4, 3, 1024, 128),...  143 us
    pallas_call x1, Pallas kernels, per_device(): pl.pallas_call(outer, grid=(LAYERS,), out_shape=(jax.ShapeDtypeStruct((3,...  4.51 us

profile of v3, /device:TPU:1, one launch (start us, length us, event | category | flops | bytes accessed | tf_op | source)
XLA Modules:
  0.0 148.0 jit_solution(15798696909068926855)
XLA Ops:
  0.6 142.9 %shard_map.68 = (bf16[4,3,1024,128]{3,2,1,0:T(8,128)(2,1)}, bf16[4,2,64,256]{3,2,1,0:T(8,128)(2,1)}, f32[1,128]{1,0:T(1,128)}) custom-call(s32[3]{0:T(128)} %sel.1, bf16[2,128,1024]{2,1,0:T(8,128)(2,1)} %feat_h.1, bf16[128,128]{1,0:T(8,128)(2,1)} %tgt_h.1, bf16[3,1024,1024]{2,1,0:T(8,128)(2,1)} %w_h.1, bf16[1024,2048]{1,0:T(8,128)(2,1)} %head_h.1), custom_call_target="tpu_custom_call" | custom-call | tf_op jit(solution)/shard_map/pallas_call | solution.py:706
  143.5 4.5 %shard_map.69 = (bf16[3,1024,256]{2,1,0:T(8,128)(2,1)}, f32[1,128]{1,0:T(1,128)}) custom-call(bf16[4,3,1024,128]{3,2,1,0:T(8,128)(2,1)} %get-tuple-element.7.ft, bf16[4,2,64,256]{3,2,1,0:T(8,128)(2,1)} %get-tuple-element.8.gu, f32[1,128]{1,0:T(1,128)} %get-tuple-element.9.loss), custom_call_target="tpu_custom_call" | custom-call | tf_op jit(solution)/shard_map/pallas_call | solution.py:720
